TPU v7x, 32 devices: a whole 2x2x4 slice. The times are simulated.
32 devices in a mesh: scen: 4 (over y, x), row: 4 (over z), col: 2 (over core).
Axes of the slice: x: 2, y: 2, z: 4, core: 2. Of those that a mesh axis runs over, the one named last changes fastest.
Arguments:
- border: bfloat16 [16, 4, 512, 512], P('scen', None, ('row', 'col')), may hold values from -4.5 to 4.5, as said below
- panel_border: bfloat16 [16, 512, 512], P('scen'), may hold values from -0.26516504 to 0.26516504
- kinv: bfloat16 [16, 512, 512], P('scen'), may hold values from -1 to 4, as said below
- factor: bfloat16 [2048, 4096], P(('scen', 'row'), 'col'), may hold values from -4.5 to 4.5
- root_block: float32 [2048, 512], P(('scen', 'row', 'col')), may hold values from -9 to 43, as said below
Outputs:
- panel_factor: float32 [2048, 512], P(('scen', 'row', 'col'))
Inputs may be any that keep to these rules, and one draw needn't show every extreme that they name: border[s, 0] is panel_border[s] transposed. `kinv`: each scenario's matrix is symmetric positive definite up to rounding, with eigenvalues 0.5 or more. `root_block`: its first 512 rows form a symmetric matrix; schur[0:512] is positive definite.
All inputs are finite; a program needn't handle non-finite values.
Results may differ from a plain program's by a relative error of at most 0.0025.
Values may be sent and summed in bfloat16 or wider, within the bound.
A program may use at most 128 MiB of HBM per device.

v0:
```python
import jax
import jax.numpy as jnp
from jax import lax
from jax.sharding import PartitionSpec as P


def spread(block, axis, owner):
    block = jnp.where(lax.axis_index(axis) == owner, block, jnp.zeros_like(block))
    return lax.psum(block, axis)


def per_device(border, panel_border, kinv, factor, root_block):
    solved = jnp.einsum(
        "snm,smp->snp", kinv, panel_border, preferred_element_type=jnp.float32
    ).astype(jnp.bfloat16)
    flat = border.reshape(border.shape[0], border.shape[1] * border.shape[2], border.shape[3])
    coupling = lax.psum_scatter(
        jnp.einsum("srn,snp->rp", flat, solved, preferred_element_type=jnp.float32),
        "scen",
        scatter_dimension=0,
        tiled=True,
    )
    heading = spread(factor, "scen", 0)
    leading = lax.all_gather(heading, "row", axis=0, tiled=True)
    update = lax.psum_scatter(
        lax.dot_general(
            factor, leading, (((1,), (1,)), ((), ())), preferred_element_type=jnp.float32
        ),
        "col",
        scatter_dimension=0,
        tiled=True,
    )
    schur = root_block + coupling - update
    assembled = lax.all_gather(schur, ("row", "col"), axis=0, tiled=True)
    diagonal_block = spread(assembled, "scen", 0)
    lower = jnp.linalg.cholesky(diagonal_block)
    return jax.scipy.linalg.solve_triangular(lower, schur.T, lower=True).T


def solution(mesh):
    in_specs = (
        P("scen", None, ("row", "col"), None),
        P("scen", None, None),
        P("scen", None, None),
        P(("scen", "row"), "col"),
        P(("scen", "row", "col"), None),
    )
    out_specs = P(("scen", "row", "col"), None)
    return jax.shard_map(
        per_device, mesh=mesh, in_specs=in_specs, out_specs=out_specs, check_vma=False
    )
```

profile of v0, /device:TPU:0, one launch (start us, length us, event | category | flops | bytes accessed | tf_op | source)
XLA Modules:
  0.0 394.9 jit_solution(12247542030386256400)
XLA Ops:
  6.5 2.0 broadcast_select_fusion.1
  8.6 49.8 %all-reduce.4.cloned.1.call-done = bf16[128,2048]{1,0:T(8,128)(2,1)} async-done(((bf16[128,2048]{1,0:T(8,128)(2,1)}), bf16[128,2048]{1,0:T(8,128)(2,1)}) %all-reduce.4.cloned.1.call-update) | async-done | bytes 524304 | tf_op jit(solution)/shard_map/psum | solution.py:9
  58.5 3.8 fusion.4
  63.4 42.5 %all-gather.3.cloned.1.call-done = bf16[512,2048]{1,0:T(8,128)(2,1)} async-done(((bf16[128,2048]{1,0:T(8,128)(2,1)}), bf16[512,2048]{1,0:T(8,128)(2,1)}) %all-gather.3.cloned.1.call-update) | async-done | bytes 2097168 | tf_op jit(solution)/shard_map/all_gather | solution.py:24
  106.0 2.3 convolution_bitcast_fusion
  109.3 23.0 %reduce-scatter.7.cloned.1.call-done = f32[64,512]{1,0:T(8,128)} async-done(((f32[256,512]{1,0:T(8,128)}), f32[64,512]{1,0:T(8,128)}) %reduce-scatter.7.cloned.1.call-update) | async-done | bytes 131088
  133.4 8.8 %reduce-scatter.9.cloned.1.call-done = f32[64,512]{1,0:T(8,128)} async-done(((f32[128,512]{1,0:T(8,128)}), f32[64,512]{1,0:T(8,128)}) %reduce-scatter.9.cloned.1.call-update) | async-done | bytes 131088
  144.3 23.2 %all-gather.5.cloned.1.call-done = f32[512,512]{1,0:T(8,128)} async-done(((f32[64,512]{1,0:T(8,128)}), f32[512,512]{1,0:T(8,128)}) %all-gather.5.cloned.1.call-update) | async-done | bytes 1048592 | tf_op jit(solution)/shard_map/all_gather | solution.py:34
  167.5 1.6 copy.18
  170.2 52.4 %all-reduce.6.cloned.1.call-done = f32[512,512]{0,1:T(8,128)} async-done(((f32[512,512]{0,1:T(8,128)}), f32[512,512]{0,1:T(8,128)}) %all-reduce.6.cloned.1.call-update) | async-done | bytes 1048592 | tf_op jit(solution)/shard_map/psum | solution.py:9
  222.6 2.7 copy.19
  225.3 1.4 fusion.7
  227.8 11.7 %cholesky.103 = f32[128,128]{1,0:T(8,128)S(1)} custom-call(f32[128,128]{1,0:T(8,128)S(1)} %cholesky.263), custom_call_target="Cholesky" | custom-call | tf_op jit(solution)/shard_map/jit(cholesky)/cholesky | solution.py:36
  239.6 9.8 %custom-call.31 = f32[1,128,128]{1,2,0:T(8,128)S(1)} custom-call(f32[1,128,128]{2,1,0:T(8,128)S(1)} %get-tuple-element.36), custom_call_target="InvertDiagBlocksLowerTriangular" | custom-call | tf_op jit(solution)/shard_map/jit(cholesky)/cholesky | solution.py:36
  251.5 1.3 convolution_subtract_fusion
  252.8 11.7 %cholesky.215 = f32[128,128]{1,0:T(8,128)S(1)} custom-call(f32[128,128]{1,0:T(8,128)S(1)} %cholesky.267), custom_call_target="Cholesky" | custom-call | tf_op jit(solution)/shard_map/jit(cholesky)/cholesky | solution.py:36
  264.6 10.6 %custom-call.32 = f32[1,128,128]{1,2,0:T(8,128)} custom-call(f32[1,128,128]{2,1,0:T(8,128)S(1)} %get-tuple-element.34), custom_call_target="InvertDiagBlocksLowerTriangular" | custom-call | tf_op jit(solution)/shard_map/jit(cholesky)/cholesky | solution.py:36
  277.6 1.5 convolution_subtract_fusion.1
  279.7 13.2 %cholesky.236 = f32[128,128]{1,0:T(8,128)} custom-call(f32[128,128]{1,0:T(8,128)} %cholesky.272), custom_call_target="Cholesky" | custom-call | tf_op jit(solution)/shard_map/jit(cholesky)/cholesky | solution.py:36
  292.9 1.6 copy.24
  294.4 1.5 select_reduce_fusion.1
  296.7 11.3 %custom-call.33 = f32[1,128,128]{1,2,0:T(8,128)} custom-call(f32[1,128,128]{2,1,0:T(8,128)} %get-tuple-element.32), custom_call_target="InvertDiagBlocksLowerTriangular" | custom-call | tf_op jit(solution)/shard_map/jit(cholesky)/cholesky | solution.py:36
  309.2 1.3 convolution_subtract_fusion.5
  310.5 11.9 %cholesky.253 = f32[128,128]{1,0:T(8,128)S(1)} custom-call(f32[128,128]{1,0:T(8,128)S(1)} %convolution_subtract_fusion.5), custom_call_target="Cholesky" | custom-call | tf_op jit(solution)/shard_map/jit(cholesky)/cholesky | solution.py:36
  328.2 14.0 %while.1 = (s32[]{:T(128)}, f32[512,512]{0,1:T(8,128)}, s32[4,2]{0,1:T(2,128)S(1)}, f32[4,128,128]{2,1,0:T(8,128)}, s32[]{:T(128)}) while((s32[]{:T(128)}, f32[512,512]{0,1:T(8,128)}, s32[4,2]{0,1:T(2,128)S(1)}, f32[4,128,128]{2,1,0:T(8,128)}, s32[]{:T(128)}) %tuple.25), condition=%wide.while_cond, body=%wide.while_body.sunk | while | flops 2 | bytes 393329 | solution.py:37
  328.8 2.2 dynamic-slice.7
  332.3 2.2 dynamic-slice.7
  335.9 2.2 dynamic-slice.7
  339.4 2.1 dynamic-slice.7
  342.3 40.1 %custom-call.34 = f32[4,128,128]{1,2,0:T(8,128)S(1)} custom-call(f32[4,128,128]{2,1,0:T(8,128)} %get-tuple-element.12), custom_call_target="InvertDiagBlocksLowerTriangular" | custom-call | tf_op jit(solution)/shard_map/jit(_solve_triangular)/triangular_solve | solution.py:37
  384.1 1.3 convolution_subtract_fusion.3
  385.7 1.4 convolution_subtract_fusion.2
  (79 shorter events, 26.0 us)
Async XLA Ops:
  6.5 52.0 %copy-start = (bf16[4,512,512]{2,1,0:T(8,128)(2,1)S(1)}, bf16[4,512,512]{2,1,0:T(8,128)(2,1)}, u32[]{:S(2)}) copy-start(bf16[4,512,512]{2,1,0:T(8,128)(2,1)} %param.7) | copy-start | bytes 6291460
  6.5 51.9 %all-reduce.4.cloned.1.call-start = ((), (), s32[]{:S(2)}) async-start(), calls=%async_computation.2 | async-start | bytes 1048576 | tf_op jit(solution)/shard_map/psum | solution.py:9
  8.6 97.4 %all-gather.3.cloned.1.call-start = ((), (), s32[]{:S(2)}) async-start(), calls=%async_computation.3 | async-start | bytes 2621440 | tf_op jit(solution)/shard_map/all_gather | solution.py:24
  58.5 73.9 %reduce-scatter.7.cloned.1.call-start = ((), (), s32[]{:S(2)}) async-start(), calls=%async_computation.6 | async-start | bytes 655360
  58.5 47.5 %copy-start.3 = (bf16[128,2048]{1,0:T(8,128)(2,1)S(1)}, bf16[128,2048]{1,0:T(8,128)(2,1)}, u32[]{:S(2)}) copy-start(bf16[128,2048]{1,0:T(8,128)(2,1)} %param.8) | copy-start | bytes 1572868
  63.4 45.8 %copy-start.5 = (f32[64,512]{1,0:T(8,128)S(1)}, f32[64,512]{1,0:T(8,128)}, u32[]{:S(2)}) copy-start(f32[64,512]{1,0:T(8,128)} %param.9) | copy-start | bytes 393220
  63.4 78.8 %reduce-scatter.9.cloned.1.call-start = ((), (), s32[]{:S(2)}) async-start(), calls=%async_computation.7 | async-start | bytes 393216
  109.1 58.4 %all-gather.5.cloned.1.call-start = ((), (), s32[]{:S(2)}) async-start(), calls=%async_computation.4 | async-start | bytes 1179648 | tf_op jit(solution)/shard_map/all_gather | solution.py:34
  144.1 78.6 %all-reduce.6.cloned.1.call-start = ((), (), s32[]{:S(2)}) async-start(), calls=%async_computation.5 | async-start | bytes 2097152 | tf_op jit(solution)/shard_map/psum | solution.py:9
  222.6 2.7 copy-start.1
  226.8 1.0 copy-start.2
  252.7 11.9 %copy-start.4 = (f32[384,128]{1,0:T(8,128)}, f32[384,128]{1,0:T(8,128)S(1)}, u32[]{:S(2)}) copy-start(f32[384,128]{1,0:T(8,128)S(1)} %convolution_subtract_fusion) | copy-start | bytes 589828
Sparse Core Ops, SparseCore 0:
  10.3 48.0 all-reduce.3
  60.0 45.9 all-gather.2
  108.8 23.5 reduce-scatter.6
  134.5 7.6 reduce-scatter.8
  144.2 23.2 all-gather.4
  170.4 52.1 all-reduce.5
where the time goes:
time: 396 us; the launch traced here: 395 us
  waiting for transfers between devices  200 us (51%)
  other arithmetic  130 us (33%)
  local copies, waits for them, and re-layouts  29.2 us (7%)
  matrix products  18.7 us (5%)
  between operations  16.3 us (4%)
    psum x2, waiting for transfers between devices, spread(): return lax.psum(block, axis)  102 us
    another operation x14, other arithmetic, per_device(): lower = jnp.linalg.cholesky(diagonal_block)  83.8 us
    all_gather x1, waiting for transfers between devices, per_device(): leading = lax.all_gather(heading, 'row', axis=0, tiled=True)  42.5 us
    another operation x3, other arithmetic, per_device(): return jax.scipy.linalg.solve_triangular(lower, schur.T, lower=True).T  41.2 us
    unnamed x8, waiting for transfers between devices  31.9 us
    all_gather x1, waiting for transfers between devices, per_device(): assembled = lax.all_gather(schur, ('row', 'col'), axis=0, tiled=True)  23.2 us
    another operation x20, local copies, waits for them, and re-layouts  14 us
  transfers between devices with their start and end apart: 6, of which 6 were waited for; matrix products, arithmetic and copies ran while one was open for 2% of the time, Pallas kernels for 0%

commit v1 on v0

v1 whole, which is shorter than its diff:
```python
import functools

import jax
import jax.numpy as jnp
from jax import lax
from jax.experimental import pallas as pl
from jax.experimental.pallas import tpu as pltpu
from jax.sharding import PartitionSpec as P

MESH = pl.DeviceIdType.MESH
F32 = jnp.float32
BLOCK = 128
STRIP = 16
SLICES = 4
HIGHEST = lax.Precision.HIGHEST


def mm(a, b, da, db, precision=None):
    return lax.dot_general(
        a, b, (((da,), (db,)), ((), ())), precision=precision, preferred_element_type=F32
    )


def panel_kernel(
    S, R, C, slices,
    border_hbm, pb_hbm, kinv_hbm, factor_hbm, root_hbm, out_ref,
    border, pb, kinv, factor, root,
    lead, roots, solved, part, part_in, cp, rs_a, dp, rs_b, diag, upd, upd_in, rest, aug, work, inv,
    in_sem, top_send, top_recv, line_send, line_recv, p_send, p_recv,
    a_send, a_recv, b_send, b_recv, g_send, g_recv, h_send, h_recv,
    l_send, l_recv, u_send, u_recv,
):
    s, r, c = lax.axis_index("scen"), lax.axis_index("row"), lax.axis_index("col")
    rows, depth = factor.shape
    own, panel = root.shape
    wide = depth // slices
    half = panel // C
    n = half // S
    blocks = panel // BLOCK
    scenarios = kinv.shape[0]
    share = scenarios // C
    groups = cp.shape[0]

    def peer_s(o):
        return lax.rem(s + o, S)

    def fetch(k):
        src, dst = (
            (factor_hbm, factor), (root_hbm, root), (pb_hbm, pb), (kinv_hbm, kinv), (border_hbm, border)
        )[k]
        return pltpu.make_async_copy(src, dst, in_sem.at[k])

    for k in range(5):
        fetch(k).start()

    barrier = pltpu.get_barrier_semaphore()
    for o in range(1, S):
        pl.semaphore_signal(barrier, inc=1, device_id=(peer_s(o), r, c), device_id_type=MESH)
    for o in range(1, R):
        pl.semaphore_signal(barrier, inc=1, device_id=(s, lax.rem(r + o, R), c), device_id_type=MESH)
    pl.semaphore_signal(barrier, inc=1, device_id=(s, r, 1 - c), device_id_type=MESH)
    pl.semaphore_wait(barrier, S + R - 1)

    def remote(src, dst, send, recv, to):
        return pltpu.make_async_remote_copy(
            src_ref=src, dst_ref=dst, send_sem=send, recv_sem=recv, device_id=to, device_id_type=MESH
        )

    def mine_of(q):
        return pl.ds(pl.multiple_of(q * rows, rows), rows)

    def top_copy(j):
        return remote(
            factor_hbm.at[:, j * wide:(j + 1) * wide], lead.at[j, mine_of(r), :],
            top_send.at[j - 1], top_recv, (j, r, c),
        )

    def line_copy(kind, q, up):
        ref = roots.at[q] if kind else lead.at[jnp.minimum(s, slices - 1), mine_of(q), :]
        return remote(
            ref, ref, line_send.at[kind, q, 1 if up else 0], line_recv.at[kind, q],
            (s, lax.rem(r + (1 if up else R - 1), R), c),
        )

    def line_start(kind, q, up):
        @pl.when(r < R - 1 if up else r > 0)
        def _():
            line_copy(kind, q, up).start()

    def hop(kind, d):
        @pl.when(s < (1 if kind else slices))
        def _():
            @pl.when(r >= d)
            def _():
                line_copy(kind, r - d, True).wait_recv()
                line_start(kind, r - d, True)

            @pl.when(r + d < R)
            def _():
                line_copy(kind, r + d, False).wait_recv()
                line_start(kind, r + d, False)

    def line_sent(kind):
        @pl.when(s < (1 if kind else slices))
        def _():
            for d in range(R):
                @pl.when(jnp.logical_and(r < R - 1, r >= d))
                def _():
                    line_copy(kind, r - d, True).wait_send()

                @pl.when(jnp.logical_and(r > 0, r + d < R))
                def _():
                    line_copy(kind, r + d, False).wait_send()

    def block(o, core):
        return pl.ds(pl.multiple_of(core * half + peer_s(o) * n, n), n)

    def p_copy(o):
        at = block(o, 1 - c)
        return remote(part.at[at, :], part_in.at[o], p_send.at[o], p_recv.at[o], (s, r, 1 - c))

    def a_copy(o):
        return remote(
            cp.at[peer_s(o)], rs_a.at[o - 1], a_send.at[o - 1], a_recv.at[o - 1], (peer_s(o), r, c)
        )

    def b_copy(o):
        return remote(
            dp.at[o], rs_b.at[o - 1], b_send.at[o - 1], b_recv.at[o - 1], (peer_s(o), r, c)
        )

    def g_copy(o):
        ref = diag.at[block(0, c), :]
        return remote(ref, ref, g_send.at[o - 1], g_recv.at[o - 1], (peer_s(o), r, c))

    def h_copy(o):
        ref = diag.at[block(S - o if o else 0, c), :]
        return remote(ref, ref, h_send.at[o], h_recv.at[o], (s, r, 1 - c))

    def l_copy(o):
        ref = lead.at[jnp.minimum(s, slices - 1)]
        return remote(
            ref, ref, l_send.at[o - 1], l_recv.at[jnp.minimum(s, slices - 1)], (peer_s(o), r, c)
        )

    u_copy = remote(upd.at[1 - c], upd_in, u_send, u_recv, (s, r, 1 - c))

    @pl.when(s == 0)
    def _():
        for j in range(1, slices):
            top_copy(j).start()
    fetch(0).wait()
    fetch(1).wait()

    @pl.when(s == 0)
    def _():
        lead[0, mine_of(r), :] = factor[:, 0:wide]
        roots[r] = root[...]
        for up in (True, False):
            line_start(0, r, up)
            line_start(1, r, up)

    @pl.when(jnp.logical_and(s > 0, s < slices))
    def _():
        top_copy(1).wait_recv()
        for up in (True, False):
            line_start(0, r, up)

    def solve(i):
        sol = mm(kinv[i], pb[i], 1, 0).astype(jnp.bfloat16)
        solved[i] = sol
        return sol

    fetch(2).wait()
    fetch(3).wait()
    for k in range(share):
        i = c * share + k
        term = mm(pb[i], solve(i), 0, 0)
        if k == 0:
            part[...] = term
        else:
            part[...] += term
        if k + 1 < R:
            hop(0, k + 1)
            hop(1, k + 1)
    for d in range(share + 1, R):
        hop(0, d)
        hop(1, d)

    @pl.when(s == 0)
    def _():
        for q in range(R):
            at = pl.ds(pl.multiple_of((q * C + c) * own, own), own)
            part[at, :] += roots[q]

    def update_half(core):
        at = pl.ds(pl.multiple_of(core * half, half), half)

        @pl.when(s < slices)
        def _():
            slot = jnp.minimum(s, slices - 1)
            part[at, :] -= mm(lead[slot, at, :], lead[slot], 1, 1)

    update_half(1 - c)
    for o in range(S):
        p_copy(o).start()
    update_half(c)
    for o in list(range(1, S)) + [0]:
        p_copy(o).wait_recv()
        dp[o] = part[block(o, c), :] + part_in[o]
        if o:
            b_copy(o).start()

    fetch(4).wait()
    for k in range(scenarios - share):
        solve(lax.rem((c + 1) * share + k, scenarios))
    for g in range(groups):
        acc = mm(border[0, g], solved[0], 1, 0)
        for i in range(1, scenarios):
            acc += mm(border[i, g], solved[i], 1, 0)
        cp[g] = acc

    total = dp[0]
    for o in range(1, S):
        b_copy(o).wait_recv()
        total += rs_b[o - 1]
    diag[block(0, c), :] = total
    for o in range(1, S):
        g_copy(o).start()
    h_copy(0).start()
    for o in range(1, S):
        a_copy(o).start()

    @pl.when(s < slices)
    def _():
        for o in range(1, S):
            l_copy(o).start()

    for o in range(1, S):
        g_copy(o).wait_recv()
        h_copy(o).start()
    for o in range(S):
        h_copy(o).wait_recv()

    down = lax.broadcasted_iota(jnp.int32, (BLOCK, BLOCK), 0)
    across = lax.broadcasted_iota(jnp.int32, (BLOCK, BLOCK), 1)
    eye = jnp.where(down == across, 1.0, 0.0).astype(F32)
    aug[...] = diag[...].T

    @pl.loop(0, blocks)
    def _(J):
        @pl.when(J == blocks - 1)
        def _():
            for j in range(slices):
                @pl.when(s != j)
                def _():
                    remote(lead.at[j], lead.at[j], l_send.at[0], l_recv.at[j], (s, r, 1 - c)).wait_recv()
            product = mm(factor[:, 0:wide], lead[0], 1, 1)
            for j in range(1, slices):
                product += mm(factor[:, j * wide:(j + 1) * wide], lead[j], 1, 1)
            for q in range(C):
                upd[q] = product[q * own:(q + 1) * own]
            u_copy.start()
            acc = root[...] + cp[s]
            for o in range(1, S):
                a_copy(o).wait_recv()
                acc += rs_a[o - 1]
            rest[...] = acc

        at = pl.ds(pl.multiple_of(J * BLOCK, BLOCK), BLOCK)
        square = aug[at, at]
        work[:, 0:BLOCK] = jnp.where(down <= across, square, square.T)
        work[:, BLOCK:2 * BLOCK] = eye
        factor_block(work)
        inv[J] = work[:, BLOCK:2 * BLOCK]
        for j in range(blocks - 1):
            @pl.when(J == j)
            def _():
                lo, hi = j * BLOCK, (j + 1) * BLOCK
                across_rows = mm(inv[j], aug[lo:hi, hi:], 1, 0, HIGHEST)
                aug[lo:hi, hi:] = across_rows
                for i in range(j + 1, blocks):
                    at_i = (i - j - 1) * BLOCK
                    aug[i * BLOCK:(i + 1) * BLOCK, i * BLOCK:] -= mm(
                        across_rows[:, at_i:at_i + BLOCK], across_rows[:, at_i:], 0, 0, HIGHEST
                    )

    u_copy.wait()
    rest[...] -= upd[c] + upd_in[...]
    for j in range(blocks):
        lo, hi = j * BLOCK, (j + 1) * BLOCK
        solution_block = mm(rest[:, lo:hi], inv[j], 1, 1, HIGHEST)
        out_ref[:, lo:hi] = solution_block
        if hi < panel:
            rest[:, hi:] -= mm(solution_block, aug[lo:hi, hi:], 1, 0, HIGHEST)

    @pl.when(s == 0)
    def _():
        for j in range(1, slices):
            top_copy(j).wait_send()

    @pl.when(s < slices)
    def _():
        for o in range(1, S):
            l_copy(o).wait_send()

    line_sent(0)
    line_sent(1)
    for o in range(S):
        p_copy(o).wait_send()
        h_copy(o).wait_send()
    for o in range(1, S):
        a_copy(o).wait_send()
        b_copy(o).wait_send()
        g_copy(o).wait_send()


def panel_step(S, R, C, border, panel_border, kinv, factor, root):
    rows, depth = factor.shape
    own, panel = root.shape
    groups = border.shape[1]
    n = panel // C // S
    slices = min(S, SLICES)
    dma = pltpu.SemaphoreType.DMA
    bf16 = jnp.bfloat16
    vmem = pltpu.VMEM
    inputs = (border, panel_border, kinv, factor, root)
    return pl.pallas_call(
        functools.partial(panel_kernel, S, R, C, slices),
        out_shape=jax.ShapeDtypeStruct((own, panel), F32),
        in_specs=[pl.BlockSpec(memory_space=pl.ANY)] * len(inputs),
        out_specs=pl.BlockSpec(memory_space=pltpu.VMEM),
        scratch_shapes=[vmem(x.shape, x.dtype) for x in inputs] + [
            vmem((slices, R * rows, depth // slices), bf16),
            vmem((R, own, panel), F32),
            vmem(kinv.shape, bf16),
            vmem((panel, panel), F32),
            vmem((S, n, panel), F32),
            vmem((groups, own, panel), F32),
            vmem((S - 1, own, panel), F32),
            vmem((S, n, panel), F32),
            vmem((S - 1, n, panel), F32),
            vmem((panel, panel), F32),
            vmem((C, own, panel), F32),
            vmem((own, panel), F32),
            vmem((own, panel), F32),
            vmem((panel, panel), F32),
            vmem((BLOCK, 2 * BLOCK), F32),
            vmem((panel // BLOCK, BLOCK, BLOCK), F32),
            dma((len(inputs),)),
            dma((slices - 1,)), dma,
            dma((2, R, 2)), dma((2, R)),
            dma((S,)), dma((S,)),
            dma((S - 1,)), dma((S - 1,)),
            dma((S - 1,)), dma((S - 1,)),
            dma((S - 1,)), dma((S - 1,)),
            dma((S,)), dma((S,)),
            dma((S - 1,)), dma((slices,)),
            dma, dma,
        ],
        compiler_params=pltpu.CompilerParams(
            collective_id=0, has_side_effects=True, vmem_limit_bytes=56 * 1024 * 1024
        ),
    )(*inputs)


def factor_block(work):
    size = work.shape[0]
    sub = lax.broadcasted_iota(jnp.int32, (STRIP, BLOCK), 0)
    for j in range(size // STRIP):
        lo = j * STRIP
        left = work[lo:lo + STRIP, 0:BLOCK]
        right = work[lo:lo + STRIP, BLOCK:2 * BLOCK]
        cols = [
            jnp.broadcast_to(left[:, lo + b:lo + b + 1], (STRIP, BLOCK)) for b in range(STRIP)
        ]
        scale = jnp.zeros((STRIP, BLOCK), F32)
        for k in range(STRIP):
            pivot = jnp.broadcast_to(cols[k][k:k + 1, :], (STRIP, BLOCK))
            inverse = pl.reciprocal(pivot, approx=True)
            inverse = inverse * (2.0 - pivot * inverse)
            scale = jnp.where(sub == k, lax.rsqrt(pivot), scale)
            if k + 1 < STRIP:
                times = jnp.where(sub > k, cols[k] * inverse, 0.0)
                for b in range(k + 1, STRIP):
                    cols[b] = cols[b] - times * cols[b][k:k + 1, :]
                left = left - times * left[k:k + 1, :]
                right = right - times * right[k:k + 1, :]
        left = left * scale
        right = right * scale
        work[lo:lo + STRIP, 0:BLOCK] = left
        work[lo:lo + STRIP, BLOCK:2 * BLOCK] = right
        if lo + STRIP < size:
            both = jnp.concatenate([left, right], axis=1)
            work[lo + STRIP:, :] -= mm(left, both, 0, 0, HIGHEST)[lo + STRIP:, :]


def solution(mesh):
    S, R, C = mesh.shape["scen"], mesh.shape["row"], mesh.shape["col"]
    in_specs = (
        P("scen", None, ("row", "col"), None),
        P("scen", None, None),
        P("scen", None, None),
        P(("scen", "row"), "col"),
        P(("scen", "row", "col"), None),
    )
    out_specs = P(("scen", "row", "col"), None)

    def per_device(border, panel_border, kinv, factor, root_block):
        return panel_step(S, R, C, border, panel_border, kinv, factor, root_block)

    return jax.shard_map(
        per_device, mesh=mesh, in_specs=in_specs, out_specs=out_specs, check_vma=False
    )
```

time: 396 us -> 80.3 us (0.20)
  waiting for transfers between devices: 200 us -> 0 us
  other arithmetic: 130 us -> 0 us
  Pallas kernels: 0 us -> 78.6 us
  local copies, waits for them, and re-layouts: 29.2 us -> 1.57 us
  matrix products: 18.7 us -> 0 us
  between operations: 16.3 us -> 0.01 us
    another operation x17 -> x0, other arithmetic: 125 us -> none  [the longest x14 83.8 us: per_device(): lower = jnp.linalg.cholesky(diagonal_block)]
    psum x2 -> x0, waiting for transfers between devices: 102 us -> none  [spread(): return lax.psum(block, axis)]
    pallas_call x0 -> x1, Pallas kernels: none -> 78.6 us  [panel_step(): pl.pallas_call(functools.partial(panel_kernel, S, R, C, slices), out_shap...]
    all_gather x2 -> x0, waiting for transfers between devices: 65.7 us -> none  [the longest x1 42.5 us: per_device(): leading = lax.all_gather(heading, 'row', axis=0, tiled=True)]
    unnamed x8 -> x0, waiting for transfers between devices: 31.9 us -> none
    another operation x34 -> x0, local copies, waits for them, and re-layouts: 19.2 us -> none
    another operation x13 -> x0, matrix products: 12.6 us -> none  [the longest x6 7.65 us: per_device(): lower = jnp.linalg.cholesky(diagonal_block)]
    dot_general x2 -> x0, matrix products: 6.15 us -> none  [the longest x1 3.85 us: per_device(): jnp.einsum('srn,snp->rp', flat, solved, preferred_element_type=jnp.float32)]
  transfers between devices with their start and end apart: 6 -> 0, of which waited for: 6 -> 0; matrix products, arithmetic and copies ran while one was open for 2% -> 0% of each run, Pallas kernels for 0% -> 0%
where the time goes in v1:
time: 80.3 us; the launch traced here: 80.2 us
  Pallas kernels  78.6 us (98%)
  local copies, waits for them, and re-layouts  1.57 us (2%)
    pallas_call x1, Pallas kernels, panel_step(): pl.pallas_call(functools.partial(panel_kernel, S, R, C, slices), out_shap...  78.6 us

profile of v1, /device:TPU:0, one launch (start us, length us, event | category | flops | bytes accessed | tf_op | source)
XLA Modules:
  0.0 80.2 jit_solution(13036985517746227570)
XLA Ops:
  0.0 78.6 %shard_map.55 = f32[64,512]{1,0:T(8,128)} custom-call(bf16[4,4,64,512]{3,2,1,0:T(8,128)(2,1)} %border_hbm.1, bf16[4,512,512]{2,1,0:T(8,128)(2,1)} %pb_hbm.1, bf16[4,512,512]{2,1,0:T(8,128)(2,1)} %kinv_hbm.1, bf16[128,2048]{1,0:T(8,128)(2,1)} %factor_hbm.1, f32[64,512]{1,0:T(8,128)} %root_hbm.1), custom_call_target="tpu_custom_call" | custom-call | tf_op jit(solution)/shard_map/pallas_call | solution.py:328
  78.6 1.6 %copy.7 = f32[64,512]{1,0:T(8,128)} copy(f32[64,512]{1,0:T(8,128)} %shard_map.55) | data formatting | bytes 262144
